TPU v7x, 512 devices: a whole 4x4x16 slice. The times are simulated.
512 devices in a mesh: dp: 2 (over core), fsdp: 32 (over y, z_lo), tensor: 8 (over z_hi, x).
Axes of the slice: x: 4, y: 4, z: 16 (z_hi: 2, z_lo: 8; z = z_hi * 8 + z_lo), core: 2. Of those that a mesh axis runs over, the one named last changes fastest.
Arguments:
- tokens: bfloat16 [16384, 4096], P(('dp', 'fsdp', 'tensor')), may hold values from -40 to 40
- norm_gain: float32 [4096], replicated, may hold values from 0.5 to 1.5
- tile_values: bfloat16 [512, 128, 128], P(('fsdp', 'tensor')), may hold values from -0.25 to 0.25
- tile_rows: int32 [8, 64], P('tensor'), may hold values from 0 to 31, as said below
- tile_cols: int32 [8, 64], P('tensor'), may hold values from 0 to 13
- tile_counts: int32 [8, 32], P('tensor'), may hold values from 0 to 2, as said below
- grad_out: bfloat16 [16384, 14336], P(('dp', 'fsdp'), 'tensor'), may hold values from -3 to 3
Outputs:
- mixed: bfloat16 [16384, 14336], P(('dp', 'fsdp'), 'tensor')
- grad_x: bfloat16 [16384, 4096], P(('dp', 'fsdp', 'tensor'))
- grad_gain: float32 [4096], replicated
- grad_tiles: float32 [512, 128, 128], P(('fsdp', 'tensor'))
Inputs may be any that keep to these rules, and one draw needn't show every extreme that they name: `tile_counts`: for each tensor index the counts over the 32 fsdp shards sum to 56, and some shard holds exactly 2. `tile_rows`: within one tensor index the (row, column) pairs of held slots are all different.
All inputs are finite; a program needn't handle non-finite values.
Results may differ from a plain program's by a relative error of at most 0.013.
Values may be sent and summed in bfloat16 or wider, within the bound.
A program may use at most 128 MiB of HBM per device.

v0:
```python
import jax
import jax.numpy as jnp
from jax import lax
from jax.sharding import PartitionSpec as P


def tile_forward(group_rows, values, rows_list, cols_list, col_tiles):
    tile_size = values.shape[1]
    blocks = group_rows.reshape(group_rows.shape[0], -1, tile_size)
    picked = jnp.take(blocks, rows_list, axis=1)
    product = jnp.einsum("tsk,skn->tsn", picked, values, preferred_element_type=jnp.float32)
    placed = (
        jnp.zeros((group_rows.shape[0], col_tiles, tile_size), jnp.float32)
        .at[:, cols_list]
        .add(product)
    )
    return placed.reshape(group_rows.shape[0], col_tiles * tile_size)


def tile_backward(grad_rows, values, rows_list, cols_list, row_tiles):
    tile_size = values.shape[1]
    blocks = grad_rows.reshape(grad_rows.shape[0], -1, tile_size)
    picked = jnp.take(blocks, cols_list, axis=1)
    product = jnp.einsum("tsn,skn->tsk", picked, values, preferred_element_type=jnp.float32)
    placed = (
        jnp.zeros((grad_rows.shape[0], row_tiles, tile_size), jnp.float32)
        .at[:, rows_list]
        .add(product)
    )
    return placed.reshape(grad_rows.shape[0], row_tiles * tile_size)


def per_device(tokens, norm_gain, tile_values, tile_rows, tile_cols, tile_counts, grad_out):
    tile_size = tile_values.shape[1]
    slot_cap = tile_values.shape[0]
    row_tiles = tokens.shape[1] // tile_size
    col_tiles = grad_out.shape[1] // tile_size
    rows_list = tile_rows[0]
    cols_list = tile_cols[0]
    shard_counts = tile_counts[0]
    held_all = (jnp.arange(slot_cap)[None, :] < shard_counts[:, None]).reshape(-1)
    own_held = jnp.arange(slot_cap) < shard_counts[lax.axis_index("fsdp")]
    local_float = tokens.astype(jnp.float32)
    inv_rms = lax.rsqrt(jnp.mean(local_float * local_float, axis=1, keepdims=True) + 1e-05)
    scaled = local_float * inv_rms
    normed = (scaled * norm_gain).astype(jnp.bfloat16)
    group_rows = lax.all_gather(normed, "tensor", axis=0, tiled=True)
    gathered = lax.all_gather(tile_values, "fsdp", axis=0, tiled=True)
    kept_values = jnp.where(held_all[:, None, None], gathered, jnp.zeros_like(gathered))
    outputs = tile_forward(group_rows, kept_values, rows_list, cols_list, col_tiles)
    mixed = outputs.astype(jnp.bfloat16)
    input_grad = lax.psum_scatter(
        tile_backward(grad_out, kept_values, rows_list, cols_list, row_tiles).astype(jnp.bfloat16),
        "tensor",
        scatter_dimension=0,
        tiled=True,
    ).astype(jnp.float32)
    x_blocks = group_rows.reshape(group_rows.shape[0], row_tiles, tile_size)
    g_blocks = grad_out.reshape(grad_out.shape[0], col_tiles, tile_size)
    picked_x = jnp.take(x_blocks, rows_list, axis=1)
    picked_g = jnp.take(g_blocks, cols_list, axis=1)
    grad_shard = lax.psum_scatter(
        jnp.einsum("tsk,tsn->skn", picked_x, picked_g, preferred_element_type=jnp.float32),
        "fsdp",
        scatter_dimension=0,
        tiled=True,
    )
    grad_shard = jnp.where(own_held[:, None, None], grad_shard, jnp.zeros_like(grad_shard))
    grad_tiles = lax.psum(grad_shard, "dp")
    gain_part = jnp.sum(input_grad * scaled, axis=0)
    grad_gain = lax.psum(gain_part, ("dp", "fsdp", "tensor"))
    hidden_grad = input_grad * norm_gain
    grad_x = (
        inv_rms * (hidden_grad - scaled * jnp.mean(hidden_grad * scaled, axis=1, keepdims=True))
    ).astype(jnp.bfloat16)
    return (mixed, grad_x, grad_gain, grad_tiles)


def solution(mesh):
    placed = (
        P(("dp", "fsdp", "tensor"), None),
        P(),
        P(("fsdp", "tensor"), None, None),
        P("tensor", None),
        P("tensor", None),
        P("tensor", None),
        P(("dp", "fsdp"), "tensor"),
    )
    return jax.shard_map(
        per_device,
        mesh=mesh,
        in_specs=placed,
        out_specs=(
            P(("dp", "fsdp"), "tensor"),
            P(("dp", "fsdp", "tensor"), None),
            P(),
            P(("fsdp", "tensor"), None, None),
        ),
        check_vma=False,
    )
```

profile of v0, /device:TPU:1, one launch (start us, length us, event | category | flops | bytes accessed | tf_op | source)
XLA Modules:
  0.0 848.5 jit_solution(9026113694259479338)
XLA Ops:
  7.9 1.5 copy.32
  11.6 3.1 gather_fusion.1
  14.7 207.7 %all-gather.3.cloned.1.call-done = bf16[64,128,128]{2,1,0:T(8,128)(2,1)} async-done(((bf16[2,128,128]{2,1,0:T(8,128)(2,1)}), bf16[64,128,128]{2,1,0:T(8,128)(2,1)}) %all-gather.3.cloned.1.call-update) | async-done | bytes 2097168 | tf_op jit(solution)/shard_map/all_gather | solution.py:48
  222.3 7.4 fusion.2
  229.8 2.4 broadcast_in_dim.57
  232.2 19.4 %scatter_fusion.1 = f32[256,32,128]{2,0,1:T(8,128)} fusion(f32[256,32,128]{2,0,1:T(8,128)} %broadcast_in_dim.57, s32[64]{0:T(128)S(1)} %fusion.18, f32[64,256,128]{2,1,0:T(8,128)} %fusion.2), kind=kCustom, calls=%fused_computation.3 | custom fusion | flops 2097152 | bytes 25166080 | tf_op jit(solution)/shard_map/scatter-add | solution.py:28
  251.6 2.5 convert_element_type.28
  254.1 2.9 copy.34
  257.0 4.1 copy.39
  261.4 162.8 %reduce-scatter.7.cloned.1.call-done = bf16[32,4096]{1,0:T(8,128)(2,1)} async-done(((bf16[256,4096]{1,0:T(8,128)(2,1)}), bf16[32,4096]{1,0:T(8,128)(2,1)}) %reduce-scatter.7.cloned.1.call-update) | async-done | bytes 262160 | tf_op jit(solution)/shard_map/reduce_scatter | solution.py:52
  425.5 1.9 fusion.12
  427.6 109.9 %all-gather.5.cloned.1.call-done = bf16[256,4096]{1,0:T(8,128)(2,1)} async-done(((bf16[32,4096]{1,0:T(8,128)(2,1)}), bf16[256,4096]{1,0:T(8,128)(2,1)}) %all-gather.5.cloned.1.call-update) | async-done | bytes 2097168 | tf_op jit(solution)/shard_map/all_gather | solution.py:47
  537.5 4.1 copy.29
  541.6 3.2 copy.30
  544.8 3.0 gather_fusion
  547.8 7.0 fusion
  556.7 103.2 %psum.14 = f32[4096]{0:T(1024)} all-reduce(f32[4096]{0:T(1024)S(1)} %get-tuple-element.18), channel_id=1, replica_groups=mesh['dp'=2,'fsdp'=32,'tensor'=8] {'dp','fsdp','tensor'}, use_global_device_ids=true, to_apply=%region_6.9 | all-reduce | flops 4096 | bytes 32768 | tf_op jit(solution)/shard_map/psum | solution.py:71
  659.9 119.5 %reduce-scatter.5.cloned.1.call-done = f32[2,128,128]{2,1,0:T(8,128)} async-done(((f32[64,128,128]{2,1,0:T(8,128)}), f32[2,128,128]{2,1,0:T(8,128)}) %reduce-scatter.5.cloned.1.call-update) | async-done | bytes 131088 | tf_op jit(solution)/shard_map/reduce_scatter | solution.py:62
  779.5 1.6 broadcast_select_fusion.9
  781.1 6.7 fusion.5
  788.0 12.4 %scatter_fusion = f32[256,14,128]{2,0,1:T(8,128)S(1)} fusion(f32[256,14,128]{2,0,1:T(8,128)S(1)} %broadcast_in_dim.54, s32[64]{0:T(128)S(1)} %fusion.17, f32[64,256,128]{2,1,0:T(8,128)} %fusion.5), kind=kCustom, calls=%fused_computation.2 | custom fusion | flops 2097152 | bytes 25166080 | tf_op jit(solution)/shard_map/scatter-add | solution.py:15
  801.2 1.4 copy.37
  802.5 37.8 %all-reduce.2.cloned.1.call-done = f32[2,128,128]{2,1,0:T(8,128)} async-done(((f32[2,128,128]{2,1,0:T(8,128)}), f32[2,128,128]{2,1,0:T(8,128)}) %all-reduce.2.cloned.1.call-update) | async-done | bytes 131088 | tf_op jit(solution)/shard_map/psum | solution.py:69
  840.4 1.6 copy.44
  (41 shorter events, 7.2 us)
Async XLA Ops:
  7.2 215.2 %all-gather.3.cloned.1.call-start = ((), (), s32[]{:S(2)}) async-start(), calls=%async_computation.2 | async-start | bytes 2162688 | tf_op jit(solution)/shard_map/all_gather | solution.py:48
  7.9 416.4 %reduce-scatter.7.cloned.1.call-start = ((), (), s32[]{:S(2)}) async-start(), calls=%async_computation.6 | async-start | bytes 2359296 | tf_op jit(solution)/shard_map/reduce_scatter | solution.py:52
  11.6 3.1 copy-start.4
  11.6 3.1 copy-start.5
  257.0 4.2 copy-start.1
  257.0 167.2 %copy-start.2 = (f32[4096]{0:T(1024)S(1)}, f32[4096]{0:T(1024)}, u32[]{:S(2)}) copy-start(f32[4096]{0:T(1024)} %param.12) | copy-start | bytes 49156
  261.2 276.3 %all-gather.5.cloned.1.call-start = ((), (), s32[]{:S(2)}) async-start(), calls=%async_computation.3 | async-start | bytes 2359296 | tf_op jit(solution)/shard_map/all_gather | solution.py:47
  427.5 352.0 %reduce-scatter.5.cloned.1.call-start = ((), (), s32[]{:S(2)}) async-start(), calls=%async_computation.4 | async-start | bytes 4325376 | tf_op jit(solution)/shard_map/reduce_scatter | solution.py:62
  554.8 0.7 copy-start.3
  554.8 226.3 %copy-start = (bf16[64,128,128]{2,1,0:T(8,128)(2,1)S(1)}, bf16[64,128,128]{2,1,0:T(8,128)(2,1)}, u32[]{:S(2)}) copy-start(bf16[64,128,128]{2,1,0:T(8,128)(2,1)} %all-gather.3.cloned.1.call-done) | copy-start | bytes 6291460
  554.9 285.5 %all-reduce.2.cloned.1.call-start = ((), (), s32[]{:S(2)}) async-start(), calls=%async_computation.5 | async-start | bytes 262144 | tf_op jit(solution)/shard_map/psum | solution.py:69
Sparse Core Ops, SparseCore 0:
  10.1 212.2 all-gather.2
  261.3 162.8 reduce-scatter.6
  428.5 108.9 all-gather.4
  555.0 224.4 reduce-scatter.4
  783.0 57.3 all-reduce.1
where the time goes:
time: 849 us; the launch traced here: 848 us
  waiting for transfers between devices  639 us (75%)
  blocking collectives  103 us (12%)
  other arithmetic  41.6 us (5%)
  local copies, waits for them, and re-layouts  29.9 us (4%)
  matrix products  21.2 us (2%)
  between operations  13.9 us (2%)
    all_gather x1, waiting for transfers between devices, per_device(): gathered = lax.all_gather(tile_values, 'fsdp', axis=0, tiled=True)  208 us
    reduce_scatter x1, waiting for transfers between devices, per_device(): lax.psum_scatter(tile_backward(grad_out, kept_values, rows_list, cols_lis...  163 us
    reduce_scatter x1, waiting for transfers between devices, per_device(): lax.psum_scatter(jnp.einsum('tsk,tsn->skn', picked_x, picked_g, preferred...  120 us
    all_gather x1, waiting for transfers between devices, per_device(): group_rows = lax.all_gather(normed, 'tensor', axis=0, tiled=True)  110 us
    psum x1, blocking collectives, per_device(): grad_gain = lax.psum(gain_part, ('dp', 'fsdp', 'tensor'))  103 us
    psum x1, waiting for transfers between devices, per_device(): grad_tiles = lax.psum(grad_shard, 'dp')  37.8 us
    scatter-add x1, other arithmetic, tile_backward(): placed = jnp.zeros((grad_rows.shape[0], row_tiles, tile_size), jnp.float3...  19.4 us
  transfers between devices with their start and end apart: 5, of which 5 were waited for; matrix products, arithmetic and copies ran while one was open for 3% of the time, Pallas kernels for 0%

commit v1 on v0

--- a/solution.py
+++ b/solution.py
@@ -66,7 +66,7 @@
         tiled=True,
     )
     grad_shard = jnp.where(own_held[:, None, None], grad_shard, jnp.zeros_like(grad_shard))
-    grad_tiles = lax.psum(grad_shard, "dp")
+    grad_tiles = jnp.sum(lax.all_gather(grad_shard, "dp"), axis=0)
     gain_part = jnp.sum(input_grad * scaled, axis=0)
     grad_gain = lax.psum(gain_part, ("dp", "fsdp", "tensor"))
     hidden_grad = input_grad * norm_gain

time: 849 us -> 817 us (0.962)
  waiting for transfers between devices: 639 us -> 580 us
  blocking collectives: 103 us -> 131 us
    psum x1 -> x0, waiting for transfers between devices: 37.8 us -> none  [per_device(): grad_tiles = lax.psum(grad_shard, 'dp')]
    all_gather x0 -> x1, blocking collectives: none -> 27.3 us  [per_device(): grad_tiles = jnp.sum(lax.all_gather(grad_shard, 'dp'), axis=0)]
    reduce_scatter x1, waiting for transfers between devices: 120 us -> 98.2 us  [per_device(): lax.psum_scatter(jnp.einsum('tsk,tsn->skn', picked_x, picked_g, preferred...]
  transfers between devices with their start and end apart: 5 -> 4, of which waited for: 5 -> 4; matrix products, arithmetic and copies ran while one was open for 3% -> 4% of each run, Pallas kernels for 0% -> 0%
where the time goes in v1:
time: 817 us; the launch traced here: 816 us
  waiting for transfers between devices  580 us (71%)
  blocking collectives  131 us (16%)
  other arithmetic  41.6 us (5%)
  local copies, waits for them, and re-layouts  28.4 us (3%)
  matrix products  21.2 us (3%)
  between operations  13.9 us (2%)
    all_gather x1, waiting for transfers between devices, per_device(): gathered = lax.all_gather(tile_values, 'fsdp', axis=0, tiled=True)  208 us
    reduce_scatter x1, waiting for transfers between devices, per_device(): lax.psum_scatter(tile_backward(grad_out, kept_values, rows_list, cols_lis...  164 us
    all_gather x1, waiting for transfers between devices, per_device(): group_rows = lax.all_gather(normed, 'tensor', axis=0, tiled=True)  110 us
    psum x1, blocking collectives, per_device(): grad_gain = lax.psum(gain_part, ('dp', 'fsdp', 'tensor'))  103 us
    reduce_scatter x1, waiting for transfers between devices, per_device(): lax.psum_scatter(jnp.einsum('tsk,tsn->skn', picked_x, picked_g, preferred...  98.2 us
    all_gather x1, blocking collectives, per_device(): grad_tiles = jnp.sum(lax.all_gather(grad_shard, 'dp'), axis=0)  27.3 us
    scatter-add x1, other arithmetic, tile_backward(): placed = jnp.zeros((grad_rows.shape[0], row_tiles, tile_size), jnp.float3...  19.4 us
  transfers between devices with their start and end apart: 4, of which 4 were waited for; matrix products, arithmetic and copies ran while one was open for 4% of the time, Pallas kernels for 0%

profile of v1, /device:TPU:1, one launch (start us, length us, event | category | flops | bytes accessed | tf_op | source)
XLA Modules:
  0.0 815.9 jit_solution(13245853512142414644)
XLA Ops:
  7.9 1.5 copy.32
  11.6 3.1 gather_fusion.1
  14.7 207.7 %all-gather.4.cloned.1.call-done = bf16[64,128,128]{2,1,0:T(8,128)(2,1)} async-done(((bf16[2,128,128]{2,1,0:T(8,128)(2,1)}), bf16[64,128,128]{2,1,0:T(8,128)(2,1)}) %all-gather.4.cloned.1.call-update) | async-done | bytes 2097168 | tf_op jit(solution)/shard_map/all_gather | solution.py:48
  222.3 7.4 fusion.2
  229.8 2.4 broadcast_in_dim.57
  232.2 19.4 %scatter_fusion.1 = f32[256,32,128]{2,0,1:T(8,128)} fusion(f32[256,32,128]{2,0,1:T(8,128)} %broadcast_in_dim.57, s32[64]{0:T(128)S(1)} %fusion.18, f32[64,256,128]{2,1,0:T(8,128)} %fusion.2), kind=kCustom, calls=%fused_computation.3 | custom fusion | flops 2097152 | bytes 25166080 | tf_op jit(solution)/shard_map/scatter-add | solution.py:28
  251.6 2.5 convert_element_type.28
  254.1 2.9 copy.34
  257.0 4.2 copy.39
  261.4 163.5 %reduce-scatter.7.cloned.1.call-done = bf16[32,4096]{1,0:T(8,128)(2,1)} async-done(((bf16[256,4096]{1,0:T(8,128)(2,1)}), bf16[32,4096]{1,0:T(8,128)(2,1)}) %reduce-scatter.7.cloned.1.call-update) | async-done | bytes 262160 | tf_op jit(solution)/shard_map/reduce_scatter | solution.py:52
  425.0 1.3 fusion.16
  426.3 1.9 fusion.12
  428.3 109.9 %all-gather.6.cloned.1.call-done = bf16[256,4096]{1,0:T(8,128)(2,1)} async-done(((bf16[32,4096]{1,0:T(8,128)(2,1)}), bf16[256,4096]{1,0:T(8,128)(2,1)}) %all-gather.6.cloned.1.call-update) | async-done | bytes 2097168 | tf_op jit(solution)/shard_map/all_gather | solution.py:47
  538.2 4.1 copy.29
  542.2 3.2 copy.30
  545.5 3.0 gather_fusion
  548.5 7.0 fusion
  557.4 103.3 %psum.7 = f32[4096]{0:T(1024)} all-reduce(f32[4096]{0:T(1024)S(1)} %get-tuple-element.18), channel_id=1, replica_groups=mesh['dp'=2,'fsdp'=32,'tensor'=8] {'dp','fsdp','tensor'}, use_global_device_ids=true, to_apply=%region_6.9 | all-reduce | flops 4096 | bytes 32768 | tf_op jit(solution)/shard_map/psum | solution.py:71
  660.7 6.7 fusion.5
  667.6 12.4 %scatter_fusion = f32[256,14,128]{2,0,1:T(8,128)S(1)} fusion(f32[256,14,128]{2,0,1:T(8,128)S(1)} %broadcast_in_dim.54, s32[64]{0:T(128)S(1)} %fusion.17, f32[64,256,128]{2,1,0:T(8,128)} %fusion.5), kind=kCustom, calls=%fused_computation.2 | custom fusion | flops 2097152 | bytes 25166080 | tf_op jit(solution)/shard_map/scatter-add | solution.py:15
  680.8 1.4 copy.37
  682.2 98.2 %reduce-scatter.5.cloned.1.call-done = f32[2,128,128]{2,1,0:T(8,128)} async-done(((f32[64,128,128]{2,1,0:T(8,128)}), f32[2,128,128]{2,1,0:T(8,128)}) %reduce-scatter.5.cloned.1.call-update) | async-done | bytes 131088 | tf_op jit(solution)/shard_map/reduce_scatter | solution.py:62
  780.4 1.0 broadcast_select_fusion.9
  781.4 27.3 %all-gather = f32[4,128,128]{2,1,0:T(8,128)S(1)} all-gather(f32[2,128,128]{2,1,0:T(8,128)S(1)} %broadcast_select_fusion.9), channel_id=2, replica_groups=mesh['dp'=2,'fsdp'=32,'tensor'=8] {'dp'}, dimensions={0}, use_global_device_ids=true | all-gather | bytes 393216 | tf_op jit(solution)/shard_map/all_gather | solution.py:69
  (39 shorter events, 6.6 us)
Async XLA Ops:
  7.2 215.2 %all-gather.4.cloned.1.call-start = ((), (), s32[]{:S(2)}) async-start(), calls=%async_computation.2 | async-start | bytes 2162688 | tf_op jit(solution)/shard_map/all_gather | solution.py:48
  7.9 417.1 %reduce-scatter.7.cloned.1.call-start = ((), (), s32[]{:S(2)}) async-start(), calls=%async_computation.5 | async-start | bytes 2359296 | tf_op jit(solution)/shard_map/reduce_scatter | solution.py:52
  11.6 3.1 copy-start.4
  11.6 3.1 copy-start.5
  257.0 4.2 copy-start.1
  257.0 168.0 %copy-start.2 = (f32[4096]{0:T(1024)S(1)}, f32[4096]{0:T(1024)}, u32[]{:S(2)}) copy-start(f32[4096]{0:T(1024)} %param.12) | copy-start | bytes 49156
  261.2 277.0 %all-gather.6.cloned.1.call-start = ((), (), s32[]{:S(2)}) async-start(), calls=%async_computation.3 | async-start | bytes 2359296 | tf_op jit(solution)/shard_map/all_gather | solution.py:47
  428.2 352.1 %reduce-scatter.5.cloned.1.call-start = ((), (), s32[]{:S(2)}) async-start(), calls=%async_computation.4 | async-start | bytes 4325376 | tf_op jit(solution)/shard_map/reduce_scatter | solution.py:62
  555.5 0.7 copy-start.3
  555.5 105.2 %copy-start = (bf16[64,128,128]{2,1,0:T(8,128)(2,1)S(1)}, bf16[64,128,128]{2,1,0:T(8,128)(2,1)}, u32[]{:S(2)}) copy-start(bf16[64,128,128]{2,1,0:T(8,128)(2,1)} %all-gather.4.cloned.1.call-done) | copy-start | bytes 6291460
Sparse Core Ops, SparseCore 0:
  10.1 212.2 all-gather.3
  261.3 163.6 reduce-scatter.6
  429.3 108.8 all-gather.5
  555.7 224.6 reduce-scatter.4
